TPU v7x, 512 devices: a whole 4x8x8 slice. The times are simulated.
512 devices in a mesh: sec: 32 (over x, y), head: 16 (over z, core).
Axes of the slice: x: 4, y: 8, z: 8, core: 2. Of those that a mesh axis runs over, the one named last changes fastest.
Arguments:
- tokens: bfloat16 [32768, 2048], P('sec', 'head'), may hold values from -6 to 6
- fresh_tokens: bfloat16 [1024, 2048], P(None, 'head'), may hold values from -6 to 6
- route_rows: int32 [32, 4, 128], P('sec'), may hold values from 0 to 255, as said below
- block_list: int32 [32, 4, 16], P('sec'), may hold values from 0 to 31, all different within a row
- norm_gain: float32 [32, 2048], P('sec'), may hold values from 0.25 to 1.75
- route_weight: bfloat16 [32, 2048], P('sec'), may hold values from -0.125 to 0.125
- w_query: bfloat16 [32, 2048, 2048], P('sec', None, 'head'), may hold values from -0.125 to 0.125
- w_key: bfloat16 [32, 2048, 2048], P('sec', None, 'head'), may hold values from -0.26367188 to 0.26367188
- w_value: bfloat16 [32, 2048, 2048], P('sec', None, 'head'), may hold values from -0.125 to 0.125
- w_out: bfloat16 [32, 2048, 2048], P('sec', None, 'head'), may hold values from -0.52734375 to 0.52734375
- cache_keys: bfloat16 [32, 4096, 2048], P('sec', None, 'head'), may hold values from -2400 to 2400
- cache_values: bfloat16 [32, 4096, 2048], P('sec', None, 'head'), may hold values from -6 to 6
Outputs:
- next_input: bfloat16 [32768, 2048], P('sec', 'head')
Inputs may be any that keep to these rules, and one draw needn't show every extreme that they name: `route_rows`: within one section and group the 128 entries are distinct row numbers of the group. `block_list`: each section's group names 16 distinct blocks.
All inputs are finite; a program needn't handle non-finite values.
Results may differ from a plain program's by a relative error of at most 0.017.
Values may be sent and summed in bfloat16 or wider, within the bound.
A program may use at most 64 MiB of HBM per device.

v0:
```python
import math
import jax
import jax.numpy as jnp
from jax import lax
from jax.sharding import Mesh
from jax.sharding import PartitionSpec as P

HEAD_DIM = 64
BLOCK = 128
HEAD = ("head_0", "head_1")


def gathered_by_axis(shard, axes, dim):
    if not axes:
        return shard
    nearer = lax.all_gather(shard, axes[-1], axis=dim, tiled=True)
    return gathered_by_axis(nearer, axes[:-1], dim)


def shifted_2(shard, axis, by):
    length = lax.axis_size(axis)
    pairs = [(i, i + by) for i in range(length) if 0 <= i + by < length]
    return lax.ppermute(shard, axis, pairs)


def attend_local(queries, key_rows, value_rows, row_index, cache_k, cache_v, picks):
    row_count, head_count, head_width = queries.shape
    group_count = picks.shape[0]
    score_scale = 1.0 / math.sqrt(head_width)
    chosen_keys = cache_k.reshape(-1, BLOCK, head_count, head_width)[picks].reshape(
        group_count, -1, head_count, head_width
    )
    chosen_values = cache_v.reshape(-1, BLOCK, head_count, head_width)[picks].reshape(
        group_count, -1, head_count, head_width
    )
    query_groups = queries.reshape(group_count, -1, head_count, head_width)
    cache_scores = (
        jnp.einsum("crhd,ckhd->chrk", query_groups, chosen_keys, preferred_element_type=jnp.float32)
        * score_scale
    )
    local_scores = (
        jnp.einsum("qhd,khd->hqk", queries, key_rows, preferred_element_type=jnp.float32)
        * score_scale
    )
    visible = row_index[None, :] <= row_index[:, None]
    local_scores = jnp.where(visible[None], local_scores, -jnp.inf)
    cache_max = jnp.transpose(jnp.max(cache_scores, axis=-1), (1, 0, 2)).reshape(
        head_count, row_count
    )
    row_max = jnp.maximum(cache_max, jnp.max(local_scores, axis=-1))
    group_max = jnp.transpose(row_max.reshape(head_count, group_count, -1), (1, 0, 2))
    cache_weights = jnp.exp(cache_scores - group_max[..., None])
    local_weights = jnp.exp(local_scores - row_max[..., None])
    cache_sum = jnp.transpose(jnp.sum(cache_weights, axis=-1), (1, 0, 2)).reshape(
        head_count, row_count
    )
    denom_sum = cache_sum + jnp.sum(local_weights, axis=-1)
    from_cache = jnp.einsum(
        "chrk,ckhd->crhd",
        cache_weights.astype(jnp.bfloat16),
        chosen_values,
        preferred_element_type=jnp.float32,
    ).reshape(row_count, head_count, head_width)
    from_local = jnp.einsum(
        "hqk,khd->qhd",
        local_weights.astype(jnp.bfloat16),
        value_rows,
        preferred_element_type=jnp.float32,
    )
    attended = (from_cache + from_local) / jnp.transpose(denom_sum)[:, :, None]
    return attended.astype(jnp.bfloat16).reshape(row_count, head_count * head_width)


def body(
    tokens,
    fresh_tokens,
    route_rows,
    block_list,
    norm_gain,
    route_weight,
    w_query,
    w_key,
    w_value,
    w_out,
    cache_keys,
    cache_values,
):
    group_count = route_rows.shape[1]
    group_rows = tokens.shape[0] // group_count
    row_index = (
        route_rows[0] + group_rows * jnp.arange(group_count, dtype=jnp.int32)[:, None]
    ).reshape(-1)
    own_rows = jnp.take(tokens, row_index, axis=0)
    picked_rows = gathered_by_axis(own_rows, HEAD, 1)
    picked = picked_rows.astype(jnp.float32)
    mean_square = jnp.mean(picked * picked, axis=-1, keepdims=True)
    normed = (picked * lax.rsqrt(mean_square + 1e-05) * norm_gain[0][None, :]).astype(jnp.bfloat16)
    gate_value = jax.nn.sigmoid(
        jnp.dot(normed, route_weight[0], preferred_element_type=jnp.float32)
    )
    local_heads = w_query.shape[2] // HEAD_DIM
    queries = (
        jnp.dot(normed, w_query[0], preferred_element_type=jnp.float32)
        .astype(jnp.bfloat16)
        .reshape(-1, local_heads, HEAD_DIM)
    )
    key_rows = (
        jnp.dot(normed, w_key[0], preferred_element_type=jnp.float32)
        .astype(jnp.bfloat16)
        .reshape(-1, local_heads, HEAD_DIM)
    )
    value_rows = (
        jnp.dot(normed, w_value[0], preferred_element_type=jnp.float32)
        .astype(jnp.bfloat16)
        .reshape(-1, local_heads, HEAD_DIM)
    )
    attended = attend_local(
        queries, key_rows, value_rows, row_index, cache_keys[0], cache_values[0], block_list[0]
    )
    output_rows = w_out[0]
    branch = jnp.dot(
        lax.all_gather(attended, HEAD, axis=1, tiled=True),
        output_rows,
        preferred_element_type=jnp.float32,
    )
    own_columns = jnp.take(tokens, row_index, axis=0).astype(jnp.float32)
    updated = (own_columns + gate_value[:, None] * branch).astype(jnp.bfloat16)
    result = tokens.at[row_index].set(updated)
    shifted = shifted_2(result, "sec", 1)
    return jnp.where(lax.axis_index("sec") == 0, fresh_tokens, shifted)


def solution(mesh):
    torus = Mesh(mesh.devices.reshape(mesh.shape["sec"], 8, 2), ("sec", "head_0", "head_1"))
    in_specs = (
        P("sec", HEAD),
        P(None, HEAD),
        P("sec", None, None),
        P("sec", None, None),
        P("sec", None),
        P("sec", None),
        P("sec", None, HEAD),
        P("sec", None, HEAD),
        P("sec", None, HEAD),
        P("sec", None, HEAD),
        P("sec", None, HEAD),
        P("sec", None, HEAD),
    )
    out_specs = P("sec", HEAD)
    return jax.shard_map(body, mesh=torus, in_specs=in_specs, out_specs=out_specs, check_vma=False)
```

profile of v0, /device:TPU:2, one launch (start us, length us, event | category | flops | bytes accessed | tf_op | source)
XLA Modules:
  0.0 152.1 jit_solution(10076083262525095151)
XLA Ops:
  8.4 1.3 gather_fusion.2
  9.9 2.1 %all_gather.9 = bf16[512,256]{1,0:T(8,128)(2,1)} all-gather(bf16[512,128]{1,0:T(8,128)(2,1)S(1)} %broadcast_select_fusion.1), channel_id=1, replica_groups=mesh['sec'=32,'head_0'=8,'head_1'=2] {'head_1'}, dimensions={1}, use_global_device_ids=true | all-gather | bytes 393216 | tf_op jit(solution)/shard_map/all_gather | solution.py:16
  12.2 1.8 %reshape.212 = bf16[32,128,2,64]{3,2,1,0:T(2,128)(2,1)} reshape(bf16[1,4096,128]{2,1,0:T(8,128)(2,1)S(1)} %copy-done.4) | data formatting | bytes 2097152 | tf_op jit(solution)/shard_map/reshape;squeeze | solution.py:30
  14.0 5.0 %copy.37 = bf16[32,128,2,64]{1,3,2,0:T(8,128)(2,1)S(1)} copy(bf16[32,128,2,64]{3,2,1,0:T(2,128)(2,1)} %reshape.212) | data formatting | bytes 2097152 | tf_op jit(solution)/shard_map/reshape;squeeze | solution.py:30
  19.1 2.1 %gather_fusion.1 = bf16[64,128,2,64]{1,3,2,0:T(8,128)(2,1)} fusion(bf16[32,128,2,64]{1,3,2,0:T(8,128)(2,1)S(1)} %copy.37, s32[1024]{0:T(1024)S(1)} %pad_clamp_fusion), kind=kCustom, calls=%fused_computation.2 | custom fusion | bytes 4194560 | tf_op jit(solution)/shard_map/gather | solution.py:30
  21.2 2.9 %copy.38 = bf16[64,128,2,64]{1,0,3,2:T(8,128)(2,1)S(1)} copy(bf16[64,128,2,64]{1,3,2,0:T(8,128)(2,1)} %gather_fusion.1) | data formatting | bytes 4194304 | tf_op jit(solution)/shard_map/gather | solution.py:30
  24.1 2.0 %reshape.161 = bf16[4,2048,2,64]{1,0,3,2:T(4,128)(2,1)} reshape(bf16[64,128,2,64]{1,0,3,2:T(8,128)(2,1)S(1)} %copy.38) | data formatting | bytes 4194304 | tf_op jit(solution)/shard_map/reshape | solution.py:30
  26.2 5.0 %reshape.211 = bf16[32,128,2,64]{3,2,1,0:T(2,128)(2,1)} reshape(bf16[1,4096,128]{2,1,0:T(8,128)(2,1)} %param.25) | data formatting | bytes 2097152 | tf_op jit(solution)/shard_map/reshape;squeeze | solution.py:33
  31.2 5.1 %copy.34 = bf16[32,128,2,64]{1,3,2,0:T(8,128)(2,1)S(1)} copy(bf16[32,128,2,64]{3,2,1,0:T(2,128)(2,1)} %reshape.211) | data formatting | bytes 2097152 | tf_op jit(solution)/shard_map/reshape;squeeze | solution.py:33
  36.2 2.1 %gather_fusion = bf16[64,128,2,64]{1,3,2,0:T(8,128)(2,1)} fusion(bf16[32,128,2,64]{1,3,2,0:T(8,128)(2,1)S(1)} %copy.34, s32[1024]{0:T(1024)S(1)} %pad_clamp_fusion), kind=kCustom, calls=%fused_computation.1 | custom fusion | bytes 4194560 | tf_op jit(solution)/shard_map/gather | solution.py:33
  38.4 3.0 %copy.35 = bf16[64,128,2,64]{1,0,3,2:T(8,128)(2,1)S(1)} copy(bf16[64,128,2,64]{1,3,2,0:T(8,128)(2,1)} %gather_fusion) | data formatting | bytes 4194304 | tf_op jit(solution)/shard_map/gather | solution.py:33
  41.4 2.1 %reshape.160 = bf16[4,2048,2,64]{1,0,3,2:T(4,128)(2,1)} reshape(bf16[64,128,2,64]{1,0,3,2:T(8,128)(2,1)S(1)} %copy.35) | data formatting | bytes 4194304 | tf_op jit(solution)/shard_map/reshape | solution.py:33
  43.7 23.5 %all-gather.3.cloned.1.call-done = bf16[512,2048]{1,0:T(8,128)(2,1)} async-done(((bf16[512,256]{1,0:T(8,128)(2,1)}), bf16[512,2048]{1,0:T(8,128)(2,1)}) %all-gather.3.cloned.1.call-update) | async-done | bytes 2097168 | tf_op jit(solution)/shard_map/all_gather | solution.py:16
  67.2 2.2 %fusion.2 = f32[512]{0:T(512)S(1)} fusion(bf16[512,2048]{1,0:T(8,128)(2,1)} %all-gather.3.cloned.1.call-done), kind=kLoop, calls=%fused_computation.10 | loop fusion | flops 3145216 | bytes 2099200 | tf_op jit(solution)/shard_map/reduce_sum | solution.py:96
  70.9 2.0 %convolution_convert_fusion.1 = bf16[512,128]{0,1:T(8,128)(2,1)S(1)} fusion(bf16[512,2048]{1,0:T(8,128)(2,1)S(1)} %fusion.4, bf16[1,2048,128]{2,1,0:T(8,128)(2,1)} %param.21), kind=kOutput, calls=%fused_computation.32 | convolution fusion | flops 268500992 | bytes 2752512 | tf_op jit(solution)/shard_map/dot_general | solution.py:108
  72.9 3.4 %multiply_reduce_fusion = (f32[4,2,128]{2,1,0:T(2,128)S(1)}, f32[4,2,128,2048]{3,2,1,0:T(8,128)S(1)}) fusion(bf16[4,2048,2,64]{1,0,3,2:T(4,128)(2,1)S(1)} %copy-done.2, bf16[4,128,2,64]{1,0,3,2:T(4,128)(2,1)S(1)} %reshape_reshape.3), kind=kOutput, calls=%fused_computation.5 | convolution fusion | flops 272628736 | bytes 10620928 | tf_op jit(solution)/shard_map/crhd,ckhd->chrk/dot_general | solution.py:38
  78.2 1.6 %fusion = f32[4,2,128]{2,1,0:T(2,128)S(1)} fusion(f32[4,2,128,2048]{3,2,1,0:T(8,128)S(1)} %get-tuple-element.11, f32[4,2,128]{2,1,0:T(2,128)S(1)} %fusion.37), kind=kLoop, calls=%fused_computation.6 | loop fusion | flops 6290432 | bytes 8396800 | tf_op jit(solution)/shard_map/reduce_sum | solution.py:54
  79.9 3.6 %fusion.18 = f32[4,2,8,8,128]{4,3,2,1,0:T(8,128)S(1)} fusion(f32[4,2,128,2048]{3,2,1,0:T(8,128)S(1)} %get-tuple-element.11, f32[4,2,128]{2,1,0:T(2,128)S(1)} %fusion.37, bf16[4,2048,2,64]{1,0,3,2:T(4,128)(2,1)S(1)} %copy-done.1), kind=kOutput, calls=%fused_computation.29 | convolution fusion | flops 274726912 | bytes 10752000 | tf_op jit(solution)/shard_map/chrk,ckhd->crhd/dot_general | solution.py:58
  84.0 1.4 fusion.24
  86.2 41.6 %all-gather.5.cloned.1.call-done = bf16[512,2048]{0,1:T(8,128)(2,1)} async-done(((bf16[512,128]{0,1:T(8,128)(2,1)}), bf16[512,2048]{0,1:T(8,128)(2,1)}) %all-gather.5.cloned.1.call-update) | async-done | bytes 2097168 | tf_op jit(solution)/shard_map/all_gather | solution.py:122
  127.7 2.4 %fusion.23 = bf16[512,128]{1,0:T(8,128)(2,1)S(1)} fusion(bf16[512,2048]{0,1:T(8,128)(2,1)} %all-gather.5.cloned.1.call-done, bf16[1,2048,128]{2,1,0:T(8,128)(2,1)} %param.23, bf16[512,128]{1,0:T(8,128)(2,1)S(1)} %broadcast_select_fusion.1, f32[512]{0:T(512)S(1)} %add_divide_fusion), kind=kOutput, calls=%fused_computation.30 | convolution fusion | flops 268697600 | bytes 2885632 | tf_op jit(solution)/shard_map/dot_general | solution.py:121
  130.2 1.9 %scatter_fusion = bf16[1024,128]{1,0:T(8,128)(2,1)S(1)} fusion(bf16[1024,128]{1,0:T(8,128)(2,1)S(1)} %copy.65, s32[512]{0:T(512)S(1)} %bitcast.90, bf16[512,128]{1,0:T(8,128)(2,1)S(1)} %fusion.23), kind=kCustom, calls=%fused_computation.3 | custom fusion | bytes 395264 | tf_op jit(solution)/shard_map/scatter | solution.py:128
  132.1 3.4 %collective-permute-start = (bf16[1024,128]{1,0:T(8,128)(2,1)S(1)}, bf16[1024,128]{1,0:T(8,128)(2,1)S(1)}, u32[]{:S(2)}, u32[]{:S(2)}) collective-permute-start(bf16[1024,128]{1,0:T(8,128)(2,1)S(1)} %scatter_fusion), channel_id=1, source_target_pairs={{0,16},{16,32},{32,48},{48,64},{64,80},{80,96},{96,112},{112,128},... | collective-permute-start | bytes 786440 | tf_op jit(solution)/shard_map/ppermute | solution.py:23
  135.5 9.1 %collective-permute-done = bf16[1024,128]{1,0:T(8,128)(2,1)S(1)} collective-permute-done((bf16[1024,128]{1,0:T(8,128)(2,1)S(1)}, bf16[1024,128]{1,0:T(8,128)(2,1)S(1)}, u32[]{:S(2)}, u32[]{:S(2)}) %collective-permute-start) | collective-permute-done | bytes 262176 | tf_op jit(solution)/shard_map/ppermute | solution.py:23
  (51 shorter events, 7.7 us)
Async XLA Ops:
  6.5 63.5 %copy-start = (bf16[1,2048,128]{2,1,0:T(8,128)(2,1)S(1)}, bf16[1,2048,128]{2,1,0:T(8,128)(2,1)}, u32[]{:S(2)}) copy-start(bf16[1,2048,128]{2,1,0:T(8,128)(2,1)} %param.20) | copy-start | bytes 1572868
  6.5 5.5 %copy-start.10 = (s32[1,4,16]{2,1,0:T(4,128)S(1)}, s32[1,4,16]{2,1,0:T(4,128)}, u32[]{:S(2)}) copy-start(s32[1,4,16]{2,1,0:T(4,128)} %param.17) | copy-start | bytes 772
  6.5 5.7 %copy-start.4 = (bf16[1,4096,128]{2,1,0:T(8,128)(2,1)S(1)}, bf16[1,4096,128]{2,1,0:T(8,128)(2,1)}, u32[]{:S(2)}) copy-start(bf16[1,4096,128]{2,1,0:T(8,128)(2,1)} %param.24) | copy-start | bytes 3145732
  6.5 60.7 %all-gather.3.cloned.1.call-start = ((), (), s32[]{:S(2)}) async-start(), calls=%async_computation | async-start | bytes 2359296 | tf_op jit(solution)/shard_map/all_gather | solution.py:16
  12.0 115.7 %all-gather.5.cloned.1.call-start = ((), (), s32[]{:S(2)}) async-start(), calls=%async_computation.1 | async-start | bytes 2228224 | tf_op jit(solution)/shard_map/all_gather | solution.py:122
  43.5 26.0 %copy-start.7 = (f32[1,2048]{1,0:T(1,128)S(1)}, f32[1,2048]{1,0:T(1,128)}, u32[]{:S(2)}) copy-start(f32[1,2048]{1,0:T(1,128)} %param.18) | copy-start | bytes 24580
  67.2 2.2 %copy-start.3 = (bf16[512,2048]{1,0:T(8,128)(2,1)S(1)}, bf16[512,2048]{1,0:T(8,128)(2,1)}, u32[]{:S(2)}) copy-start(bf16[512,2048]{1,0:T(8,128)(2,1)} %all-gather.3.cloned.1.call-done) | copy-start | bytes 6291460
  70.9 2.0 %copy-start.2 = (bf16[4,2048,2,64]{1,0,3,2:T(4,128)(2,1)S(1)}, bf16[4,2048,2,64]{1,0,3,2:T(4,128)(2,1)}, u32[]{:S(2)}) copy-start(bf16[4,2048,2,64]{1,0,3,2:T(4,128)(2,1)} %reshape.161) | copy-start | bytes 6291460
  76.3 1.0 copy-start.5
  78.2 1.7 %copy-start.1 = (bf16[4,2048,2,64]{1,0,3,2:T(4,128)(2,1)S(1)}, bf16[4,2048,2,64]{1,0,3,2:T(4,128)(2,1)}, u32[]{:S(2)}) copy-start(bf16[4,2048,2,64]{1,0,3,2:T(4,128)(2,1)} %reshape.160) | copy-start | bytes 6291460
  84.0 1.5 copy-start.9
  84.0 1.5 copy-start.8
  86.2 58.4 %copy-start.6 = (bf16[1024,128]{1,0:T(8,128)(2,1)S(1)}, bf16[1024,128]{1,0:T(8,128)(2,1)}, u32[]{:S(2)}) copy-start(bf16[1024,128]{1,0:T(8,128)(2,1)} %param.15) | copy-start | bytes 786436
  132.1 12.5 %collective-permute-start = (bf16[1024,128]{1,0:T(8,128)(2,1)S(1)}, bf16[1024,128]{1,0:T(8,128)(2,1)S(1)}, u32[]{:S(2)}, u32[]{:S(2)}) collective-permute-start(bf16[1024,128]{1,0:T(8,128)(2,1)S(1)} %scatter_fusion), channel_id=1, source_target_pairs={{0,16},{16,32},{32,48},{48,64},{64,80},{80,96},{96,112},{112,128},... | collective-permute-start | bytes 786440 | tf_op jit(solution)/shard_map/ppermute | solution.py:23
Sparse Core Ops, SparseCore 0:
  12.2 55.0 all-gather.2
  85.5 42.1 all-gather.4
where the time goes:
time: 153 us; the launch traced here: 152 us
  waiting for transfers between devices  74.2 us (48%)
  local copies, waits for them, and re-layouts  36.2 us (24%)
  matrix products  15.7 us (10%)
  between operations  13.7 us (9%)
  other arithmetic  6.82 us (4%)
  starting transfers between devices  3.44 us (2%)
  blocking collectives  2.13 us (1%)
    all_gather x1, waiting for transfers between devices, body(): lax.all_gather(attended, HEAD, axis=1, tiled=True)  41.6 us
    all_gather x1, waiting for transfers between devices, gathered_by_axis(): nearer = lax.all_gather(shard, axes[-1], axis=dim, tiled=True)  23.5 us
    another operation x2, local copies, waits for them, and re-layouts, attend_local(): cache_v.reshape(-1, BLOCK, head_count, head_width)[picks]  10 us
    ppermute x1, waiting for transfers between devices, shifted_2(): return lax.ppermute(shard, axis, pairs)  9.06 us
    another operation x2, local copies, waits for them, and re-layouts, attend_local(): cache_k.reshape(-1, BLOCK, head_count, head_width)[picks]  6.87 us
    gather x2, local copies, waits for them, and re-layouts, attend_local(): cache_v.reshape(-1, BLOCK, head_count, head_width)[picks]  5.13 us
    gather x2, local copies, waits for them, and re-layouts, attend_local(): cache_k.reshape(-1, BLOCK, head_count, head_width)[picks]  5.07 us
    dot_general x1, matrix products, attend_local(): jnp.einsum('chrk,ckhd->crhd', cache_weights.astype(jnp.bfloat16), chosen_...  3.63 us
  transfers between devices with their start and end apart: 3, of which 3 were waited for; matrix products, arithmetic and copies ran while one was open for 21% of the time, Pallas kernels for 0%

commit v1 on v0

--- a/solution.py
+++ b/solution.py
@@ -119,7 +119,9 @@
     )
     output_rows = w_out[0]
     branch = jnp.dot(
-        lax.all_gather(attended, HEAD, axis=1, tiled=True),
+        jnp.concatenate(
+            lax.all_to_all(jnp.stack([attended] * lax.axis_size(HEAD)), HEAD, 0, 0), axis=1
+        ),
         output_rows,
         preferred_element_type=jnp.float32,
     )

time: 153 us -> 166 us (1.085)
  waiting for transfers between devices: 74.2 us -> 81.2 us
  starting transfers between devices: 3.44 us -> 8.72 us
    all_to_all x0 -> x1, waiting for transfers between devices: none -> 48.5 us  [body(): lax.all_to_all(jnp.stack([attended] * lax.axis_size(HEAD)), HEAD, 0, 0)]
    all_gather x1 -> x0, waiting for transfers between devices: 41.6 us -> none  [body(): lax.all_gather(attended, HEAD, axis=1, tiled=True)]
    all_to_all x0 -> x1, starting transfers between devices: none -> 5.34 us  [body(): lax.all_to_all(jnp.stack([attended] * lax.axis_size(HEAD)), HEAD, 0, 0)]
  transfers between devices with their start and end apart: 3 -> 3, of which waited for: 3 -> 3; matrix products, arithmetic and copies ran while one was open for 21% -> 19% of each run, Pallas kernels for 0% -> 0%
where the time goes in v1:
time: 166 us; the launch traced here: 165 us
  waiting for transfers between devices  81.2 us (49%)
  local copies, waits for them, and re-layouts  37.6 us (23%)
  matrix products  15.1 us (9%)
  between operations  13.7 us (8%)
  starting transfers between devices  8.72 us (5%)
  other arithmetic  6.82 us (4%)
  blocking collectives  2.13 us (1%)
    all_to_all x1, waiting for transfers between devices, body(): lax.all_to_all(jnp.stack([attended] * lax.axis_size(HEAD)), HEAD, 0, 0)  48.5 us
    all_gather x1, waiting for transfers between devices, gathered_by_axis(): nearer = lax.all_gather(shard, axes[-1], axis=dim, tiled=True)  23.6 us
    another operation x2, local copies, waits for them, and re-layouts, attend_local(): cache_v.reshape(-1, BLOCK, head_count, head_width)[picks]  10 us
    ppermute x1, waiting for transfers between devices, shifted_2(): return lax.ppermute(shard, axis, pairs)  9 us
    another operation x2, local copies, waits for them, and re-layouts, attend_local(): cache_k.reshape(-1, BLOCK, head_count, head_width)[picks]  6.87 us
    all_to_all x1, starting transfers between devices, body(): lax.all_to_all(jnp.stack([attended] * lax.axis_size(HEAD)), HEAD, 0, 0)  5.34 us
    gather x2, local copies, waits for them, and re-layouts, attend_local(): cache_v.reshape(-1, BLOCK, head_count, head_width)[picks]  5.11 us
    gather x2, local copies, waits for them, and re-layouts, attend_local(): cache_k.reshape(-1, BLOCK, head_count, head_width)[picks]  5.07 us
  transfers between devices with their start and end apart: 3, of which 3 were waited for; matrix products, arithmetic and copies ran while one was open for 19% of the time, Pallas kernels for 0%

profile of v1, /device:TPU:2, one launch (start us, length us, event | category | flops | bytes accessed | tf_op | source)
XLA Modules:
  0.0 165.2 jit_solution(15996362019660396736)
XLA Ops:
  9.9 2.1 %all_gather.6 = bf16[512,256]{1,0:T(8,128)(2,1)} all-gather(bf16[512,128]{1,0:T(8,128)(2,1)S(1)} %broadcast_select_fusion.1), channel_id=1, replica_groups=mesh['sec'=32,'head_0'=8,'head_1'=2] {'head_1'}, dimensions={1}, use_global_device_ids=true | all-gather | bytes 393216 | tf_op jit(solution)/shard_map/all_gather | solution.py:16
  12.1 1.8 %reshape.218 = bf16[32,128,2,64]{3,2,1,0:T(2,128)(2,1)} reshape(bf16[1,4096,128]{2,1,0:T(8,128)(2,1)S(1)} %copy-done.4) | data formatting | bytes 2097152 | tf_op jit(solution)/shard_map/reshape;squeeze | solution.py:30
  14.0 5.0 %copy.38 = bf16[32,128,2,64]{1,3,2,0:T(8,128)(2,1)S(1)} copy(bf16[32,128,2,64]{3,2,1,0:T(2,128)(2,1)} %reshape.218) | data formatting | bytes 2097152 | tf_op jit(solution)/shard_map/reshape;squeeze | solution.py:30
  19.0 2.1 %gather_fusion.1 = bf16[64,128,2,64]{1,3,2,0:T(8,128)(2,1)} fusion(bf16[32,128,2,64]{1,3,2,0:T(8,128)(2,1)S(1)} %copy.38, s32[1024]{0:T(1024)S(1)} %pad_clamp_fusion), kind=kCustom, calls=%fused_computation.2 | custom fusion | bytes 4194560 | tf_op jit(solution)/shard_map/gather | solution.py:30
  21.2 2.9 %copy.39 = bf16[64,128,2,64]{1,0,3,2:T(8,128)(2,1)S(1)} copy(bf16[64,128,2,64]{1,3,2,0:T(8,128)(2,1)} %gather_fusion.1) | data formatting | bytes 4194304 | tf_op jit(solution)/shard_map/gather | solution.py:30
  24.1 2.0 %reshape.166 = bf16[4,2048,2,64]{1,0,3,2:T(4,128)(2,1)} reshape(bf16[64,128,2,64]{1,0,3,2:T(8,128)(2,1)S(1)} %copy.39) | data formatting | bytes 4194304 | tf_op jit(solution)/shard_map/reshape | solution.py:30
  26.2 5.0 %reshape.217 = bf16[32,128,2,64]{3,2,1,0:T(2,128)(2,1)} reshape(bf16[1,4096,128]{2,1,0:T(8,128)(2,1)} %param.25) | data formatting | bytes 2097152 | tf_op jit(solution)/shard_map/reshape;squeeze | solution.py:33
  31.1 5.1 %copy.35 = bf16[32,128,2,64]{1,3,2,0:T(8,128)(2,1)S(1)} copy(bf16[32,128,2,64]{3,2,1,0:T(2,128)(2,1)} %reshape.217) | data formatting | bytes 2097152 | tf_op jit(solution)/shard_map/reshape;squeeze | solution.py:33
  36.2 2.1 %gather_fusion = bf16[64,128,2,64]{1,3,2,0:T(8,128)(2,1)} fusion(bf16[32,128,2,64]{1,3,2,0:T(8,128)(2,1)S(1)} %copy.35, s32[1024]{0:T(1024)S(1)} %pad_clamp_fusion), kind=kCustom, calls=%fused_computation.1 | custom fusion | bytes 4194560 | tf_op jit(solution)/shard_map/gather | solution.py:33
  38.3 3.0 %copy.36 = bf16[64,128,2,64]{1,0,3,2:T(8,128)(2,1)S(1)} copy(bf16[64,128,2,64]{1,3,2,0:T(8,128)(2,1)} %gather_fusion) | data formatting | bytes 4194304 | tf_op jit(solution)/shard_map/gather | solution.py:33
  41.3 2.1 %reshape.165 = bf16[4,2048,2,64]{1,0,3,2:T(4,128)(2,1)} reshape(bf16[64,128,2,64]{1,0,3,2:T(8,128)(2,1)S(1)} %copy.36) | data formatting | bytes 4194304 | tf_op jit(solution)/shard_map/reshape | solution.py:33
  43.6 23.6 %all-gather.2.cloned.1.call-done = bf16[512,2048]{1,0:T(8,128)(2,1)} async-done(((bf16[512,256]{1,0:T(8,128)(2,1)}), bf16[512,2048]{1,0:T(8,128)(2,1)}) %all-gather.2.cloned.1.call-update) | async-done | bytes 2097168 | tf_op jit(solution)/shard_map/all_gather | solution.py:16
  67.2 2.2 %fusion.2 = f32[512]{0:T(512)S(1)} fusion(bf16[512,2048]{1,0:T(8,128)(2,1)} %all-gather.2.cloned.1.call-done), kind=kLoop, calls=%fused_computation.10 | loop fusion | flops 3145216 | bytes 2099200 | tf_op jit(solution)/shard_map/reduce_sum | solution.py:96
  70.9 2.0 %convolution_convert_fusion.1 = bf16[512,128]{0,1:T(8,128)(2,1)S(1)} fusion(bf16[512,2048]{1,0:T(8,128)(2,1)S(1)} %fusion.4, bf16[1,2048,128]{2,1,0:T(8,128)(2,1)} %param.21), kind=kOutput, calls=%fused_computation.32 | convolution fusion | flops 268500992 | bytes 2752512 | tf_op jit(solution)/shard_map/dot_general | solution.py:108
  73.0 3.4 %multiply_reduce_fusion = (f32[4,2,128]{2,1,0:T(2,128)S(1)}, f32[4,2,128,2048]{3,2,1,0:T(8,128)S(1)}) fusion(bf16[4,2048,2,64]{1,0,3,2:T(4,128)(2,1)S(1)} %copy-done.2, bf16[4,128,2,64]{1,0,3,2:T(4,128)(2,1)S(1)} %reshape_reshape.3), kind=kOutput, calls=%fused_computation.5 | convolution fusion | flops 272628736 | bytes 10620928 | tf_op jit(solution)/shard_map/crhd,ckhd->chrk/dot_general | solution.py:38
  78.2 1.6 fusion
  79.9 3.6 %fusion.18 = f32[4,2,8,8,128]{4,3,2,1,0:T(8,128)S(1)} fusion(f32[4,2,128,2048]{3,2,1,0:T(8,128)S(1)} %get-tuple-element.11, f32[4,2,128]{2,1,0:T(2,128)S(1)} %fusion.37, bf16[4,2048,2,64]{1,0,3,2:T(4,128)(2,1)S(1)} %copy-done.1), kind=kOutput, calls=%fused_computation.29 | convolution fusion | flops 274726912 | bytes 10752000 | tf_op jit(solution)/shard_map/chrk,ckhd->crhd/dot_general | solution.py:58
  84.7 1.5 stack.3
  86.3 5.3 %all-to-all-start = ((bf16[16,512,128]{1,2,0:T(8,128)(2,1)}), bf16[16,512,128]{1,2,0:T(8,128)(2,1)}, u32[]{:S(2)}, u32[]{:S(2)}) async-start(bf16[16,512,128]{1,2,0:T(8,128)(2,1)} %stack.3), calls=%async_computation | async-start | bytes 4194304 | tf_op jit(solution)/shard_map/all_to_all | solution.py:123
  92.3 48.5 %all-to-all-done = bf16[16,512,128]{1,2,0:T(8,128)(2,1)} async-done(((bf16[16,512,128]{1,2,0:T(8,128)(2,1)}), bf16[16,512,128]{1,2,0:T(8,128)(2,1)}, u32[]{:S(2)}, u32[]{:S(2)}) %all-to-all-start) | async-done | bytes 2097184 | tf_op jit(solution)/shard_map/all_to_all | solution.py:123
  140.8 2.5 %fusion.23 = bf16[512,128]{1,0:T(8,128)(2,1)S(1)} fusion(bf16[512,2048]{0,1:T(8,128)(2,1)} %bitcast.25, bf16[1,2048,128]{2,1,0:T(8,128)(2,1)} %param.23, bf16[512,128]{1,0:T(8,128)(2,1)S(1)} %broadcast_select_fusion.1, f32[512]{0:T(512)S(1)} %add_divide_fusion), kind=kOutput, calls=%fused_computation.30 | convolution fusion | flops 268697600 | bytes 2885632 | tf_op jit(solution)/shard_map/dot_general | solution.py:121
  143.3 1.9 %scatter_fusion = bf16[1024,128]{1,0:T(8,128)(2,1)S(1)} fusion(bf16[1024,128]{1,0:T(8,128)(2,1)S(1)} %copy.66, s32[512]{0:T(512)S(1)} %bitcast.93, bf16[512,128]{1,0:T(8,128)(2,1)S(1)} %fusion.23), kind=kCustom, calls=%fused_computation.3 | custom fusion | bytes 395264 | tf_op jit(solution)/shard_map/scatter | solution.py:130
  145.2 3.4 %collective-permute-start = (bf16[1024,128]{1,0:T(8,128)(2,1)S(1)}, bf16[1024,128]{1,0:T(8,128)(2,1)S(1)}, u32[]{:S(2)}, u32[]{:S(2)}) collective-permute-start(bf16[1024,128]{1,0:T(8,128)(2,1)S(1)} %scatter_fusion), channel_id=1, source_target_pairs={{0,16},{16,32},{32,48},{48,64},{64,80},{80,96},{96,112},{112,128},... | collective-permute-start | bytes 786440 | tf_op jit(solution)/shard_map/ppermute | solution.py:23
  148.6 9.0 %collective-permute-done = bf16[1024,128]{1,0:T(8,128)(2,1)S(1)} collective-permute-done((bf16[1024,128]{1,0:T(8,128)(2,1)S(1)}, bf16[1024,128]{1,0:T(8,128)(2,1)S(1)}, u32[]{:S(2)}, u32[]{:S(2)}) %collective-permute-start) | collective-permute-done | bytes 262176 | tf_op jit(solution)/shard_map/ppermute | solution.py:23
  (51 shorter events, 9.6 us)
Async XLA Ops:
  6.5 63.5 %copy-start = (bf16[1,2048,128]{2,1,0:T(8,128)(2,1)S(1)}, bf16[1,2048,128]{2,1,0:T(8,128)(2,1)}, u32[]{:S(2)}) copy-start(bf16[1,2048,128]{2,1,0:T(8,128)(2,1)} %param.20) | copy-start | bytes 1572868
  6.5 5.5 %copy-start.10 = (s32[1,4,16]{2,1,0:T(4,128)S(1)}, s32[1,4,16]{2,1,0:T(4,128)}, u32[]{:S(2)}) copy-start(s32[1,4,16]{2,1,0:T(4,128)} %param.17) | copy-start | bytes 772
  6.5 5.6 %copy-start.4 = (bf16[1,4096,128]{2,1,0:T(8,128)(2,1)S(1)}, bf16[1,4096,128]{2,1,0:T(8,128)(2,1)}, u32[]{:S(2)}) copy-start(bf16[1,4096,128]{2,1,0:T(8,128)(2,1)} %param.24) | copy-start | bytes 3145732
  6.5 60.7 %all-gather.2.cloned.1.call-start = ((), (), s32[]{:S(2)}) async-start(), calls=%async_computation.1 | async-start | bytes 2359296 | tf_op jit(solution)/shard_map/all_gather | solution.py:16
  43.4 26.1 %copy-start.7 = (f32[1,2048]{1,0:T(1,128)S(1)}, f32[1,2048]{1,0:T(1,128)}, u32[]{:S(2)}) copy-start(f32[1,2048]{1,0:T(1,128)} %param.18) | copy-start | bytes 24580
  67.2 2.2 %copy-start.3 = (bf16[512,2048]{1,0:T(8,128)(2,1)S(1)}, bf16[512,2048]{1,0:T(8,128)(2,1)}, u32[]{:S(2)}) copy-start(bf16[512,2048]{1,0:T(8,128)(2,1)} %all-gather.2.cloned.1.call-done) | copy-start | bytes 6291460
  70.9 2.0 %copy-start.2 = (bf16[4,2048,2,64]{1,0,3,2:T(4,128)(2,1)S(1)}, bf16[4,2048,2,64]{1,0,3,2:T(4,128)(2,1)}, u32[]{:S(2)}) copy-start(bf16[4,2048,2,64]{1,0,3,2:T(4,128)(2,1)} %reshape.166) | copy-start | bytes 6291460
  76.3 1.0 copy-start.5
  78.2 1.7 %copy-start.1 = (bf16[4,2048,2,64]{1,0,3,2:T(4,128)(2,1)S(1)}, bf16[4,2048,2,64]{1,0,3,2:T(4,128)(2,1)}, u32[]{:S(2)}) copy-start(bf16[4,2048,2,64]{1,0,3,2:T(4,128)(2,1)} %reshape.165) | copy-start | bytes 6291460
  86.2 5.4 %copy-start.9 = (s32[1,4,128]{2,1,0:T(4,128)S(1)}, s32[1,4,128]{2,1,0:T(4,128)}, u32[]{:S(2)}) copy-start(s32[1,4,128]{2,1,0:T(4,128)} %param.16) | copy-start | bytes 6148
  86.2 5.4 %copy-start.8 = (bf16[1,2048]{1,0:T(2,128)(2,1)S(1)}, bf16[1,2048]{1,0:T(2,128)(2,1)}, u32[]{:S(2)}) copy-start(bf16[1,2048]{1,0:T(2,128)(2,1)} %param.19) | copy-start | bytes 12292
  86.3 54.6 %all-to-all-start = ((bf16[16,512,128]{1,2,0:T(8,128)(2,1)}), bf16[16,512,128]{1,2,0:T(8,128)(2,1)}, u32[]{:S(2)}, u32[]{:S(2)}) async-start(bf16[16,512,128]{1,2,0:T(8,128)(2,1)} %stack.3), calls=%async_computation | async-start | bytes 4194304 | tf_op jit(solution)/shard_map/all_to_all | solution.py:123
  140.8 16.8 %copy-start.6 = (bf16[1024,128]{1,0:T(8,128)(2,1)S(1)}, bf16[1024,128]{1,0:T(8,128)(2,1)}, u32[]{:S(2)}) copy-start(bf16[1024,128]{1,0:T(8,128)(2,1)} %param.15) | copy-start | bytes 786436
  145.2 12.4 %collective-permute-start = (bf16[1024,128]{1,0:T(8,128)(2,1)S(1)}, bf16[1024,128]{1,0:T(8,128)(2,1)S(1)}, u32[]{:S(2)}, u32[]{:S(2)}) collective-permute-start(bf16[1024,128]{1,0:T(8,128)(2,1)S(1)} %scatter_fusion), channel_id=1, source_target_pairs={{0,16},{16,32},{32,48},{48,64},{64,80},{80,96},{96,112},{112,128},... | collective-permute-start | bytes 786440 | tf_op jit(solution)/shard_map/ppermute | solution.py:23
Sparse Core Ops, SparseCore 0:
  12.2 55.0 all-gather.1
